TPU v7x, 1024 devices: a whole 4x4x32 slice. The times are simulated.
1024 devices in a mesh: dp: 64 (over z, core), expert: 16 (over y, x).
Axes of the slice: x: 4, y: 4, z: 32, core: 2. Of those that a mesh axis runs over, the one named last changes fastest.
Arguments:
- out_grad: bfloat16 [131072, 3584], P(('dp', 'expert')), may hold values from -0.29882812 to 0.29882812
- router_input: bfloat16 [131072, 3584], P(('dp', 'expert')), may hold values from -24 to 24
- down_weight: bfloat16 [16, 1024, 3584], P('expert'), may hold values from -0.1875 to 0.1875
- saved_hidden: bfloat16 [64, 16, 16, 10, 1024], P('dp', 'expert'), may hold values from -3 to 3
- expert_ids: int32 [131072, 1], P(('dp', 'expert')), may hold values from 0 to 15; in each aligned block of 128 rows (0 to 127, 128 to 255, ...) at most 10 rows name the same one
- affinity: float32 [131072, 8], P(('dp', 'expert')), may hold values from 0.05 to 0.95
- other_dgate: float32 [131072, 7], P(('dp', 'expert')), may hold values from -6 to 6
Outputs:
- grad_hidden: bfloat16 [64, 16, 16, 10, 1024], P('dp', 'expert')
- grad_logit: float32 [131072, 8], P(('dp', 'expert'))
- grad_centroid: float32 [16, 3584], P('expert', 'dp')
Inputs may be any that keep to these rules, and one draw needn't show every extreme that they name: `expert_ids`: of the 128 tokens of one device, at most 10 name the same expert, and in every draw some expert is named by exactly 10 tokens of one device.
All inputs are finite; a program needn't handle non-finite values.
Results may differ from a plain program's by a relative error of at most 0.0049.
Values may be sent and summed in bfloat16 or wider, within the bound.
A program may use at most 32 MiB of HBM per device.

v0:
```python
import jax
import jax.numpy as jnp
from jax import lax
from jax.sharding import PartitionSpec as P

route_scale = 2.5


def body(out_grad, router_input, down_weight, saved_hidden, expert_ids, affinity, other_dgate):
    owners = lax.axis_size("expert")
    capacity = saved_hidden.shape[3]
    model_width = out_grad.shape[1]
    hidden_width = saved_hidden.shape[4]
    owner_col = expert_ids[:, 0]
    routed = owner_col[:, None] == jnp.arange(owners, dtype=jnp.int32)[None, :]
    counts = routed.astype(jnp.int32)
    earlier = (jnp.cumsum(counts, axis=0) - counts) * counts
    slot_index = jnp.sum(earlier, axis=1)
    position = owner_col * capacity + slot_index
    picking = position[None, :] == jnp.arange(owners * capacity, dtype=jnp.int32)[:, None]
    sent_rows = jnp.dot(
        picking.astype(jnp.bfloat16), out_grad, preferred_element_type=jnp.float32
    ).astype(jnp.bfloat16)
    total_aff = jnp.sum(affinity, axis=1)
    gate_value = (route_scale * affinity[:, 0] / total_aff).astype(jnp.bfloat16)
    sent_gate = jnp.sum(
        jnp.where(picking, gate_value[None, :].astype(jnp.float32), 0.0), axis=1
    ).astype(jnp.bfloat16)
    arrived_rows, arrived_gate = (
        lax.all_to_all(
            sent_rows.reshape(owners, capacity, model_width),
            "expert",
            split_axis=0,
            concat_axis=0,
            tiled=True,
        ),
        lax.all_to_all(
            sent_gate.reshape(owners, capacity), "expert", split_axis=0, concat_axis=0, tiled=True
        ),
    )
    grad_rows = lax.dot_general(
        arrived_rows.reshape(-1, model_width),
        down_weight[0],
        (((1,), (1,)), ((), ())),
        preferred_element_type=jnp.float32,
    )
    flat_hidden = saved_hidden.reshape(-1, hidden_width)
    slot_dgate = jnp.sum(flat_hidden.astype(jnp.float32) * grad_rows, axis=1)
    grad_hidden = (
        (arrived_gate.reshape(-1).astype(jnp.float32)[:, None] * grad_rows)
        .astype(jnp.bfloat16)
        .reshape(saved_hidden.shape)
    )
    returned = lax.all_to_all(
        slot_dgate.reshape(owners, capacity), "expert", split_axis=0, concat_axis=0, tiled=True
    )
    own_dgate = jnp.sum(jnp.where(picking, returned.reshape(-1)[:, None], 0.0), axis=0)
    dgate = jnp.concatenate([own_dgate[:, None], other_dgate], axis=1)
    weighted = jnp.sum(dgate * affinity, axis=1) / total_aff
    grad_logit = (
        route_scale / total_aff[:, None] * (dgate - weighted[:, None]) * affinity * (1.0 - affinity)
    )
    picked = jnp.where(routed, grad_logit[:, 0:1].astype(jnp.bfloat16), jnp.zeros((), jnp.bfloat16))
    partial_term = jnp.dot(picked.T, router_input, preferred_element_type=jnp.float32)
    half_sum = lax.psum_scatter(partial_term, "expert", scatter_dimension=0, tiled=True)
    grad_centroid = lax.psum_scatter(half_sum, "dp", scatter_dimension=1, tiled=True)
    return (grad_hidden, grad_logit, grad_centroid)


def solution(mesh):
    in_specs = (
        P(("dp", "expert"), None),
        P(("dp", "expert"), None),
        P("expert", None, None),
        P("dp", "expert", None, None, None),
        P(("dp", "expert"), None),
        P(("dp", "expert"), None),
        P(("dp", "expert"), None),
    )
    out_specs = (P("dp", "expert", None, None, None), P(("dp", "expert"), None), P("expert", "dp"))
    return jax.shard_map(body, mesh=mesh, in_specs=in_specs, out_specs=out_specs, check_vma=False)
```

profile of v0, /device:TPU:1, one launch (start us, length us, event | category | flops | bytes accessed | tf_op | source)
XLA Modules:
  0.0 428.5 jit_solution(14693375703782394626)
XLA Ops:
  7.2 0.0 copy-start
  7.2 0.8 fusion.3
  8.0 0.2 reduce_window_sum.11
  8.2 0.8 select_reduce_fusion.2
  9.0 0.7 multiply_add_fusion
  9.7 0.0 copy-done
  9.7 0.4 convolution_convert_fusion
  10.1 1.5 reshape.78
  11.6 0.0 copy-start.2
  11.6 7.7 %all-to-all-start.1 = ((bf16[16,10,3584]{2,1,0:T(8,128)(2,1)}), bf16[16,10,3584]{2,1,0:T(8,128)(2,1)S(1)}, u32[]{:S(2)}, u32[]{:S(2)}) async-start(bf16[16,10,3584]{2,1,0:T(8,128)(2,1)} %reshape.78), calls=%async_computation.1 | async-start | bytes 3670016 | tf_op jit(solution)/shard_map/all_to_all | solution.py:30
  19.3 0.0 copy-done.2
  19.3 1.2 copy.19
  20.5 1.3 reshape.82
  21.9 17.1 %all-to-all-done.1 = bf16[16,10,3584]{2,1,0:T(8,128)(2,1)S(1)} async-done(((bf16[16,10,3584]{2,1,0:T(8,128)(2,1)}), bf16[16,10,3584]{2,1,0:T(8,128)(2,1)S(1)}, u32[]{:S(2)}, u32[]{:S(2)}) %all-to-all-start.1) | async-done | bytes 1146912 | tf_op jit(solution)/shard_map/all_to_all | solution.py:30
  39.0 1.2 reshape.79
  40.2 0.0 copy-start.3
  40.2 0.0 copy-start.4
  40.2 0.0 copy-start.1
  40.2 6.1 %multiply_reduce_fusion = (f32[160]{0:T(256)S(1)}, f32[160,1024]{1,0:T(8,128)S(1)}) fusion(f32[160,1024]{1,0:T(8,128)S(1)} %reshape.82, bf16[160,3584]{1,0:T(8,128)(2,1)} %reshape.79, bf16[1,1024,3584]{2,1,0:T(8,128)(2,1)} %param.9), kind=kOutput, calls=%fused_computation.3 | convolution fusion | flops 1174732672 | bytes 9798272 | tf_op jit(solution)/shard_map/dot_general | solution.py:41
  46.4 0.7 all_to_all.15
  47.1 5.0 %all-to-all-start.2 = ((f32[16,1,10]{2,1,0:T(1,128)}), f32[16,1,10]{2,1,0:T(1,128)S(1)}, u32[]{:S(2)}, u32[]{:S(2)}) async-start(f32[16,1,10]{2,1,0:T(1,128)} %bitcast.3), calls=%async_computation.2 | async-start | bytes 16384 | tf_op jit(solution)/shard_map/all_to_all | solution.py:54
  52.1 1.3 dynamic-slice
  53.4 1.3 dynamic-slice.2
  55.4 3.1 all-to-all-done.2
  58.4 0.5 broadcast.26
  58.9 0.7 reduce.7
  59.6 0.1 broadcast_in_dim.50
  59.7 0.1 select_reduce_fusion
  59.8 0.0 copy-done.3
  59.8 0.0 copy-done.4
  59.9 0.6 fusion.11
  60.5 0.1 select_reduce_fusion.1
  60.6 0.7 convert_element_type.69
  61.3 3.6 all-to-all-start
  64.9 0.0 all-reduce.4.cloned.1.call-start
  64.9 0.0 copy-done.1
  65.0 0.0 copy-done.5
  65.0 1.1 fusion.5
  66.0 0.0 all-reduce.4.cloned.1.call-update
  66.0 5.2 %all-to-all-done = bf16[16,1,10]{2,1,0:T(2,128)(2,1)S(1)} async-done(((bf16[16,1,10]{2,1,0:T(2,128)(2,1)}), bf16[16,1,10]{2,1,0:T(2,128)(2,1)S(1)}, u32[]{:S(2)}, u32[]{:S(2)}) %all-to-all-start) | async-done | bytes 352 | tf_op jit(solution)/shard_map/all_to_all | solution.py:37
  71.3 0.1 reshape.81
  71.3 0.1 multiply_convert_fusion
  71.5 0.1 reshape.80
  71.6 0.9 copy.21
  72.5 166.3 %all-reduce.4.cloned.1.call-done = f32[16,3584]{1,0:T(8,128)} async-done(((f32[16,3584]{1,0:T(8,128)}), f32[16,3584]{1,0:T(8,128)}) %all-reduce.4.cloned.1.call-update) | async-done | bytes 229392
  238.8 1.6 constant_dynamic-slice_fusion.1
  240.4 180.7 %all-reduce.1 = f32[1,3584]{1,0:T(1,128)S(1)} all-reduce(f32[1,3584]{1,0:T(1,128)S(1)} %constant_dynamic-slice_fusion.1), channel_id=3, replica_groups=mesh['dp'=64,'expert'=16] {'dp'}, use_global_device_ids=true, to_apply=%region_8.9.clone | all-reduce | flops 3584 | bytes 28672
  421.1 0.6 constant_dynamic-slice_fusion
  (5 shorter events, 0.1 us)
Async XLA Ops:
  7.2 2.5 copy-start
  11.6 7.7 %copy-start.2 = (bf16[1,1,16,10,1024]{4,2,3,1,0:T(8,128)(2,1)S(1)}, bf16[1,1,16,10,1024]{4,2,3,1,0:T(8,128)(2,1)}, u32[]{:S(2)}) copy-start(bf16[1,1,16,10,1024]{4,2,3,1,0:T(8,128)(2,1)} %param.10) | copy-start | bytes 983044
  11.6 27.4 %all-to-all-start.1 = ((bf16[16,10,3584]{2,1,0:T(8,128)(2,1)}), bf16[16,10,3584]{2,1,0:T(8,128)(2,1)S(1)}, u32[]{:S(2)}, u32[]{:S(2)}) async-start(bf16[16,10,3584]{2,1,0:T(8,128)(2,1)} %reshape.78), calls=%async_computation.1 | async-start | bytes 3670016 | tf_op jit(solution)/shard_map/all_to_all | solution.py:30
  40.2 19.6 %copy-start.3 = (f32[128,8]{0,1:T(8,128)S(1)}, f32[128,8]{0,1:T(8,128)}, u32[]{:S(2)}) copy-start(f32[128,8]{0,1:T(8,128)} %param.12) | copy-start | bytes 12292
  40.2 19.6 %copy-start.4 = (f32[128,7]{0,1:T(8,128)S(1)}, f32[128,7]{0,1:T(8,128)}, u32[]{:S(2)}) copy-start(f32[128,7]{0,1:T(8,128)} %param.13) | copy-start | bytes 10756
  40.2 24.7 %copy-start.1 = (bf16[128,3584]{1,0:T(8,128)(2,1)S(1)}, bf16[128,3584]{1,0:T(8,128)(2,1)}, u32[]{:S(2)}) copy-start(bf16[128,3584]{1,0:T(8,128)(2,1)} %param.8) | copy-start | bytes 2752516
  40.2 24.7 %copy-start.5 = (s32[128,1]{0,1:T(1,128)S(1)}, s32[128,1]{0,1:T(1,128)}, u32[]{:S(2)}) copy-start(s32[128,1]{0,1:T(1,128)} %param.11) | copy-start | bytes 1540
  47.1 11.4 %all-to-all-start.2 = ((f32[16,1,10]{2,1,0:T(1,128)}), f32[16,1,10]{2,1,0:T(1,128)S(1)}, u32[]{:S(2)}, u32[]{:S(2)}) async-start(f32[16,1,10]{2,1,0:T(1,128)} %bitcast.3), calls=%async_computation.2 | async-start | bytes 16384 | tf_op jit(solution)/shard_map/all_to_all | solution.py:54
  61.3 9.9 %all-to-all-start = ((bf16[16,1,10]{2,1,0:T(2,128)(2,1)}), bf16[16,1,10]{2,1,0:T(2,128)(2,1)S(1)}, u32[]{:S(2)}, u32[]{:S(2)}) async-start(bf16[16,1,10]{2,1,0:T(2,128)(2,1)} %convert_element_type.69), calls=%async_computation | async-start | bytes 16384 | tf_op jit(solution)/shard_map/all_to_all | solution.py:37
  64.9 173.9 %all-reduce.4.cloned.1.call-start = ((), (), s32[]{:S(2)}) async-start(), calls=%async_computation.3 | async-start | bytes 458752
Sparse Core Ops, SparseCore 0:
  68.9 169.8 all-reduce.3
where the time goes:
time: 430 us; the launch traced here: 429 us
  waiting for transfers between devices  192 us (45%)
  blocking collectives  181 us (42%)
  starting transfers between devices  16.4 us (4%)
  between operations  14.8 us (3%)
  local copies, waits for them, and re-layouts  13.1 us (3%)
  matrix products  7.62 us (2%)
    unnamed x1, blocking collectives  181 us
    unnamed x2, waiting for transfers between devices  166 us
    all_to_all x1, waiting for transfers between devices, body(): lax.all_to_all(sent_rows.reshape(owners, capacity, model_width), 'expert'...  17.1 us
  transfers between devices with their start and end apart: 4, of which 4 were waited for; matrix products, arithmetic and copies ran while one was open for 2% of the time, Pallas kernels for 0%

commit v1 on v0

v1 whole, which is shorter than its diff:
```python
import jax
import jax.numpy as jnp
from jax import lax
from jax.experimental import pallas as pl
from jax.experimental.pallas import tpu as pltpu
from jax.sharding import PartitionSpec as P

MESH = pl.DeviceIdType.MESH
ROUTE_SCALE = 2.5
BF = jnp.bfloat16
F32 = jnp.float32
I32 = jnp.int32

SIDE = 4
E = SIDE * SIDE
CAP = 10
HEAD = 8
TOK = 128
D = 3584
FF = 1024
CW = 512
NC = D // CW
BW = CW + CW // 4
ROWS = 2 * E * HEAD
NZ = 32
OUT = 56
HALF = 64

_HOP = (0, 1, 2, 1)
_ORDER = sorted(
    [(dx, dy) for dy in range(SIDE) for dx in range(SIDE) if (dx, dy) != (0, 0)],
    key=lambda o: -(_HOP[o[0]] + _HOP[o[1]]),
)
_DX = sum(o[0] * SIDE**i for i, o in enumerate(_ORDER))
_DY = sum(o[1] * SIDE**i for i, o in enumerate(_ORDER))


def dot(a, b):
    return jnp.dot(a, b, preferred_element_type=F32)


def dot_t(a, b):
    return lax.dot_general(a, b, (((1,), (1,)), ((), ())), preferred_element_type=F32)


def iota(shape, dim):
    return lax.broadcasted_iota(I32, shape, dim)


def slot_row(i):
    j = i - E * HEAD
    main = (i % HEAD) * E + i // HEAD
    rest = (HEAD + j % 2) * E + j // HEAD
    return jnp.where(i < E * HEAD, main, rest)


def kernel(
    og_h, ri_h, w_h, hid_h, ids_h, aff_h, oth_h,
    gh_o, gl_o, gc_o,
    wv, ogv, riv, hidv, idv, affv, othv,
    hp, sel, gsum, acc, vs, vr, gs, gr, xp, p1s, p1r, zs, zr,
    wsem, lsem, vsend, vrecv, osend, orecv, s1, r1, s2, r2, up, down,
):
    dp = lax.axis_index("dp")
    me = lax.axis_index("expert")
    z, core = dp // 2, dp % 2
    x, y = me % SIDE, me // SIDE

    def at(dx, dy):
        return ((y + dy) % SIDE) * SIDE + (x + dx) % SIDE

    def level(dz):
        return ((z + dz) % NZ) * 2 + core

    def around(body):
        def step(i, c):
            cx, cy = c
            body(at(cx % SIDE, cy % SIDE))
            return cx // SIDE, cy // SIDE

        lax.fori_loop(0, E - 1, step, (jnp.int32(_DX), jnp.int32(_DY)))

    small = [
        pltpu.make_async_copy(s, d, lsem.at[i])
        for i, (s, d) in enumerate(((ids_h, idv), (aff_h, affv), (oth_h, othv), (hid_h, hidv), (ri_h, riv)))
    ]
    for copy in small[:4]:
        copy.start()

    def w_copy(c):
        return pltpu.make_async_copy(w_h.at[:, pl.ds(c * CW, CW)], wv.at[c], wsem.at[c])

    def og_copy(c):
        return pltpu.make_async_copy(og_h.at[:, pl.ds(c * CW, CW)], ogv.at[c], wsem.at[NC + c])

    for c in range(NC):
        w_copy(c).start()

    barrier = pltpu.get_barrier_semaphore()

    def greet(e):
        pl.semaphore_signal(barrier, inc=1, device_id=(dp, e), device_id_type=MESH)
        pl.semaphore_signal(barrier, inc=1, device_id=(z * 2 + 1 - core, e), device_id_type=MESH)

    around(greet)
    pl.semaphore_signal(barrier, inc=1, device_id=(z * 2 + 1 - core, me), device_id_type=MESH)
    for dz in (1, NZ - 1):
        pl.semaphore_signal(barrier, inc=1, device_id=(level(dz), me), device_id_type=MESH)

    for c in range(NC):
        og_copy(c).start()
    small[4].start()

    small[3].wait()
    place = slot_row(iota((ROWS, E * CAP), 0)) == iota((ROWS, E * CAP), 1)
    hp[...] = dot(place.astype(F32).astype(BF), hidv[...]).astype(BF)

    fold = (iota((E * HEAD, CW // 4), 0) % HEAD) // 2

    def put(buf, c, p):
        buf[c, :, :, 0:CW] = p[0 : E * HEAD].reshape(E, HEAD, CW).astype(BF)
        rest = p[E * HEAD :, 0 : CW // 4]
        for q in range(1, 4):
            rest = jnp.where(fold == q, p[E * HEAD :, q * (CW // 4) : (q + 1) * (CW // 4)], rest)
        buf[c, :, :, CW:BW] = rest.reshape(E, HEAD, CW // 4).astype(BF)

    def get(buf, c):
        main = buf[c, :, :, 0:CW].astype(F32).reshape(E * HEAD, CW).astype(BF)
        rest = buf[c, :, :, CW:BW].astype(F32).reshape(E * HEAD, CW // 4)
        rest = jnp.concatenate([jnp.where(fold == q, rest, 0.0) for q in range(4)], axis=1).astype(BF)
        return jnp.concatenate([main, rest], axis=0)

    def own_block(src, dst, c):
        dst[c, me] = src[c, me]

    def send(src, dst, ssem, rsem, c):
        def one(e):
            pltpu.make_async_remote_copy(
                src_ref=src.at[c, e], dst_ref=dst.at[c, me], send_sem=ssem, recv_sem=rsem.at[c],
                device_id=(dp, e), device_id_type=MESH,
            ).start()

        around(one)

    def arrived(buf, rsem, c):
        part = buf.at[c, pl.ds(0, E - 1)]
        pltpu.make_async_copy(part, part, rsem.at[c]).wait()

    def sent(buf, ssem):
        part = buf.at[:, pl.ds(0, E - 1)]
        pltpu.make_async_copy(part, part, ssem).wait()

    def make_v(c):
        w_copy(c).wait()
        put(vs, c, dot(hp[...], wv[c]))
        own_block(vs, vr, c)

    make_v(0)
    pl.semaphore_wait(barrier, 2 * (E - 1) + 3)
    send(vs, vr, vsend, vrecv, 0)

    @pl.loop(1, NC)
    def _(c):
        make_v(c)
        send(vs, vr, vsend, vrecv, c)

    def tell(i):
        r = 2**i
        pl.semaphore_signal(up.at[i], inc=1, device_id=(level(r), me), device_id_type=MESH)
        pl.semaphore_signal(down.at[i], inc=1, device_id=(level(NZ - r), me), device_id_type=MESH)

    def hear(i):
        pl.semaphore_wait(up.at[i], 1)
        pl.semaphore_wait(down.at[i], 1)

    tell(0)

    for i in range(3):
        small[i].wait()
    ids = idv[...]
    aff = affv[...]
    routed = (iota((E, TOK), 0) == ids).astype(F32)
    before = (iota((TOK, TOK), 0) < iota((TOK, TOK), 1)).astype(F32).astype(BF)
    earlier = dot(routed.astype(BF), before)
    slot = jnp.sum(routed * earlier, axis=0, keepdims=True)
    wanted = slot * float(E) + ids.astype(F32)
    mine = slot_row(iota((ROWS, TOK), 0)).astype(F32) == wanted
    sel[...] = mine.astype(F32)
    total = jnp.sum(aff, axis=0, keepdims=True)
    gate = (ROUTE_SCALE * aff[0:1] / total).astype(BF).astype(F32)

    small[4].wait()
    for j in range(NZ // 2):
        start = 4 * OUT * j
        low = start // 128 * 128
        off = start - low
        width = min(384, D - low) if off + 4 * OUT > 256 else 256
        lane = iota((width, 256), 1)
        source = (2 * ((lane % 128) // HALF) + lane // 128) * OUT + lane % HALF + off
        hot = (iota((width, 256), 0) == source) & (lane % HALF < OUT)
        moved = dot(riv[:, low : low + width], hot.astype(F32).astype(BF)).astype(BF)
        q, h = j // 2, j % 2
        xp[q * TOK : (q + 1) * TOK, h * 128 : (h + 1) * 128] = moved[:, 0:128]
        xp[q * TOK : (q + 1) * TOK, 256 + h * 128 : 256 + (h + 1) * 128] = moved[:, 128:256]

    hear(0)
    tell(1)

    scaled = (sel[...] * gate).astype(BF)

    @pl.loop(0, NC)
    def _(c):
        og_copy(c).wait()
        put(gs, c, dot(scaled, ogv[c]))
        own_block(gs, gr, c)

    hear(1)
    tell(2)

    gsum[...] = jnp.zeros_like(gsum)

    @pl.loop(0, NC)
    def _(c):
        arrived(vr, vrecv, c)
        gsum[...] += dot_t(get(vr, c), ogv[c])

    own = jnp.sum(gsum[...] * sel[...], axis=0, keepdims=True)
    dgate = jnp.concatenate([own, othv[...]], axis=0)
    weighted = jnp.sum(dgate * aff, axis=0, keepdims=True) / total
    grad_logit = ROUTE_SCALE / total * (dgate - weighted) * aff * (1.0 - aff)
    gl_o[...] = grad_logit

    rows = iota((E * 8, TOK), 0)
    picked = jnp.where((rows // 8) == ids, grad_logit[0:1].astype(BF).astype(F32), 0.0)
    wide = jnp.concatenate([jnp.where(rows % 8 == q, picked, 0.0).astype(BF) for q in range(8)], axis=1)
    term = dot(wide, xp[...]).reshape(E, 8, 512).astype(BF)
    p1s[0] = term[:, :, 0:256]
    p1s[1] = term[:, :, 256:512]
    index = core * E + me
    p1r[index] = p1s[core, me]

    def term_to(e, k):
        pltpu.make_async_remote_copy(
            src_ref=p1s.at[k, e], dst_ref=p1r.at[index], send_sem=s1, recv_sem=r1,
            device_id=(z * 2 + k, e), device_id_type=MESH,
        ).start()

    def term_both(e):
        term_to(e, core)
        term_to(e, 1 - core)

    around(term_both)
    term_to(me, 1 - core)

    hear(2)
    tell(3)

    part = p1r.at[pl.ds(0, 2 * E - 1)]
    pltpu.make_async_copy(part, part, r1).wait()
    plane = jnp.sum(p1r[...].astype(F32), axis=0)
    for q in range(8):
        for h in range(2):
            zs[2 * q + h] = plane[q : q + 1, h * 128 : (h + 1) * 128]
    zr[z] = zs[z // 2]

    hear(3)

    @pl.loop(0, NZ - 1)
    def _(i):
        k = (i + 1) // 2
        dz = NZ // 2 + k * (1 - 2 * (i % 2))
        to = (z + dz) % NZ
        pltpu.make_async_remote_copy(
            src_ref=zs.at[to // 2], dst_ref=zr.at[z], send_sem=s2, recv_sem=r2,
            device_id=(to * 2 + core, me), device_id_type=MESH,
        ).start()

    @pl.loop(0, NC)
    def _(c):
        send(gs, gr, osend, orecv, c)

    acc[...] = jnp.zeros_like(acc)

    @pl.loop(0, NC)
    def _(c):
        arrived(gr, orecv, c)
        acc[...] += dot_t(get(gr, c), wv[c])

    back = (slot_row(iota((E * CAP, ROWS), 1)) == iota((E * CAP, ROWS), 0)).astype(F32).astype(BF)
    high = acc[...].astype(BF)
    low = (acc[...] - high.astype(F32)).astype(BF)
    gh_o[...] = (dot(back, high) + dot(back, low)).astype(BF)

    part = zr.at[pl.ds(0, NZ - 1)]
    pltpu.make_async_copy(part, part, r2).wait()
    column = zr[0]
    for i in range(1, NZ):
        column = column + zr[i]
    gc_o[...] = jnp.where(z % 2 == 0, column[:, 0:OUT], column[:, HALF : HALF + OUT])

    sent(vs, vsend)
    sent(gs, osend)
    part = p1r.at[pl.ds(0, 2 * E - 1)]
    pltpu.make_async_copy(part, part, s1).wait()
    part = zr.at[pl.ds(0, NZ - 1)]
    pltpu.make_async_copy(part, part, s2).wait()


def body(out_grad, router_input, down_weight, saved_hidden, expert_ids, affinity, other_dgate):
    hidden = saved_hidden[0, 0].transpose(1, 0, 2).reshape(CAP * E, FF)
    vmem, dma = pltpu.VMEM, pltpu.SemaphoreType.DMA
    hbm = pl.BlockSpec(memory_space=pl.ANY)
    here = pl.BlockSpec(memory_space=pltpu.VMEM)
    block = (NC, E, HEAD, BW)
    grad_hidden, grad_logit, grad_centroid = pl.pallas_call(
        kernel,
        out_shape=(
            jax.ShapeDtypeStruct((CAP * E, FF), BF),
            jax.ShapeDtypeStruct((8, TOK), F32),
            jax.ShapeDtypeStruct((1, OUT), F32),
        ),
        in_specs=[hbm] * 7,
        out_specs=(here, here, here),
        scratch_shapes=[
            vmem((NC, FF, CW), BF), vmem((NC, TOK, CW), BF), vmem((TOK, D), BF), vmem((CAP * E, FF), BF),
            vmem((1, TOK), I32), vmem((8, TOK), F32), vmem((7, TOK), F32),
            vmem((ROWS, FF), BF), vmem((ROWS, TOK), F32), vmem((ROWS, TOK), F32), vmem((ROWS, FF), F32),
            vmem(block, BF), vmem(block, BF), vmem(block, BF), vmem(block, BF),
            vmem((8 * TOK, 512), BF),
            vmem((2, E, 8, 256), BF), vmem((2 * E, 8, 256), BF),
            vmem((NZ // 2, 1, 128), F32), vmem((NZ, 1, 128), F32),
            dma((2 * NC,)), dma((5,)), dma, dma((NC,)), dma, dma((NC,)), dma, dma, dma, dma,
            pltpu.SemaphoreType.REGULAR((4,)), pltpu.SemaphoreType.REGULAR((4,)),
        ],
        compiler_params=pltpu.CompilerParams(
            collective_id=0, has_side_effects=True, vmem_limit_bytes=56 * 1024 * 1024
        ),
    )(out_grad, router_input, down_weight[0], hidden, expert_ids.T, affinity.T, other_dgate.T)
    grad_hidden = grad_hidden.reshape(CAP, E, FF).transpose(1, 0, 2)[None, None]
    return grad_hidden, grad_logit.T, grad_centroid


def solution(mesh):
    tokens = P(("dp", "expert"), None)
    slots = P("dp", "expert", None, None, None)
    return jax.shard_map(
        body,
        mesh=mesh,
        in_specs=(tokens, tokens, P("expert", None, None), slots, tokens, tokens, tokens),
        out_specs=(slots, tokens, P("expert", "dp")),
        check_vma=False,
    )
```

time: 430 us -> 65.9 us (0.15)
  waiting for transfers between devices: 192 us -> 0 us
  blocking collectives: 181 us -> 0 us
  Pallas kernels: 0 us -> 60.9 us
  starting transfers between devices: 16.4 us -> 0 us
  between operations: 14.8 us -> 0.64 us
  local copies, waits for them, and re-layouts: 13.1 us -> 4.11 us
  matrix products: 7.62 us -> 0 us
    unnamed x1 -> x0, blocking collectives: 181 us -> none
    unnamed x2 -> x0, waiting for transfers between devices: 166 us -> none
    pallas_call x0 -> x1, Pallas kernels: none -> 60.9 us  [body(): pl.pallas_call(kernel, out_shape=(jax.ShapeDtypeStruct((CAP * E, FF), BF)...]
    all_to_all x3 -> x0, waiting for transfers between devices: 25.4 us -> none  [the longest x1 17.1 us: body(): lax.all_to_all(sent_rows.reshape(owners, capacity, model_width), 'expert'...]
    all_to_all x3 -> x0, starting transfers between devices: 16.3 us -> none  [the longest x1 7.72 us: body(): lax.all_to_all(sent_rows.reshape(owners, capacity, model_width), 'expert'...]
    dot_general x3 -> x0, matrix products: 7.62 us -> none  [the longest x1 6.12 us: body(): lax.dot_general(arrived_rows.reshape(-1, model_width), down_weight[0], ((...]
  transfers between devices with their start and end apart: 4 -> 0, of which waited for: 4 -> 0; matrix products, arithmetic and copies ran while one was open for 2% -> 0% of each run, Pallas kernels for 0% -> 0%
where the time goes in v1:
time: 65.9 us; the launch traced here: 65.6 us
  Pallas kernels  60.9 us (92%)
  local copies, waits for them, and re-layouts  4.11 us (6%)
    pallas_call x1, Pallas kernels, body(): pl.pallas_call(kernel, out_shape=(jax.ShapeDtypeStruct((CAP * E, FF), BF)...  60.9 us
    unnamed x3, local copies, waits for them, and re-layouts  4.11 us

profile of v1, /device:TPU:1, one launch (start us, length us, event | category | flops | bytes accessed | tf_op | source)
XLA Modules:
  0.0 65.6 jit_solution(12028808619774412464)
XLA Ops:
  0.6 60.9 %shard_map.94 = (bf16[160,1024]{1,0:T(8,128)(2,1)}, f32[8,128]{1,0:T(8,128)}, f32[1,56]{1,0:T(1,128)}) custom-call(bf16[128,3584]{1,0:T(8,128)(2,1)} %og_h.1, bf16[128,3584]{1,0:T(8,128)(2,1)} %ri_h.1, bf16[1024,3584]{1,0:T(8,128)(2,1)} %bitcast.15, bf16[160,1024]{1,0:T(8,128)(2,1)} %bitcast.16, s32[1,128]{1,0:T(1,128)} %bitcast.21, f32[8,128]{1,0:T(8,128)} %bitcast.18, ...), custom_call_target="tpu_custom_call" | custom-call | tf_op jit(solution)/shard_map/pallas_call | solution.py:315
  61.5 1.7 %copy.13 = bf16[1,1,16,10,1024]{4,2,3,1,0:T(8,128)(2,1)} copy(bf16[1,1,16,10,1024]{4,2,3,1,0:T(8,128)(2,1)} %bitcast.17) | data formatting | bytes 655360
  63.2 1.3 %copy.14 = f32[128,8]{0,1:T(8,128)} copy(f32[128,8]{0,1:T(8,128)} %bitcast.20) | data formatting | bytes 8192
  64.5 1.1 %copy.15 = f32[1,56]{1,0:T(1,128)} copy(f32[1,56]{1,0:T(1,128)} %get-tuple-element.14) | data formatting | bytes 448

commit v2 on v1

--- a/solution.py
+++ b/solution.py
@@ -25,14 +25,13 @@
 NZ = 32
 OUT = 56
 HALF = 64
+EARLY = 2
 
 _HOP = (0, 1, 2, 1)
 _ORDER = sorted(
     [(dx, dy) for dy in range(SIDE) for dx in range(SIDE) if (dx, dy) != (0, 0)],
     key=lambda o: -(_HOP[o[0]] + _HOP[o[1]]),
 )
-_DX = sum(o[0] * SIDE**i for i, o in enumerate(_ORDER))
-_DY = sum(o[1] * SIDE**i for i, o in enumerate(_ORDER))
 
 
 def dot(a, b):
@@ -63,22 +62,20 @@
 ):
     dp = lax.axis_index("dp")
     me = lax.axis_index("expert")
-    z, core = dp // 2, dp % 2
-    x, y = me % SIDE, me // SIDE
+    z, core = lax.div(dp, 2), lax.rem(dp, 2)
+    x, y = lax.rem(me, SIDE), lax.div(me, SIDE)
 
     def at(dx, dy):
-        return ((y + dy) % SIDE) * SIDE + (x + dx) % SIDE
+        return lax.rem(y + dy, SIDE) * SIDE + lax.rem(x + dx, SIDE)
 
     def level(dz):
-        return ((z + dz) % NZ) * 2 + core
+        return lax.rem(z + dz, NZ) * 2 + core
+
+    others = [at(dx, dy) for dx, dy in _ORDER]
 
     def around(body):
-        def step(i, c):
-            cx, cy = c
-            body(at(cx % SIDE, cy % SIDE))
-            return cx // SIDE, cy // SIDE
-
-        lax.fori_loop(0, E - 1, step, (jnp.int32(_DX), jnp.int32(_DY)))
+        for e in others:
+            body(e)
 
     small = [
         pltpu.make_async_copy(s, d, lsem.at[i])
@@ -155,15 +152,6 @@
         put(vs, c, dot(hp[...], wv[c]))
         own_block(vs, vr, c)
 
-    make_v(0)
-    pl.semaphore_wait(barrier, 2 * (E - 1) + 3)
-    send(vs, vr, vsend, vrecv, 0)
-
-    @pl.loop(1, NC)
-    def _(c):
-        make_v(c)
-        send(vs, vr, vsend, vrecv, c)
-
     def tell(i):
         r = 2**i
         pl.semaphore_signal(up.at[i], inc=1, device_id=(level(r), me), device_id_type=MESH)
@@ -173,7 +161,22 @@
         pl.semaphore_wait(up.at[i], 1)
         pl.semaphore_wait(down.at[i], 1)
 
+    make_v(0)
+    pl.semaphore_wait(barrier, 2 * (E - 1) + 3)
+    send(vs, vr, vsend, vrecv, 0)
+
     tell(0)
+
+    def more_v(c):
+        make_v(c)
+        send(vs, vr, vsend, vrecv, c)
+
+    pl.loop(1, 4)(more_v)
+    hear(0)
+    tell(1)
+    pl.loop(4, NC)(more_v)
+    hear(1)
+    tell(2)
 
     for i in range(3):
         small[i].wait()
@@ -203,9 +206,6 @@
         xp[q * TOK : (q + 1) * TOK, h * 128 : (h + 1) * 128] = moved[:, 0:128]
         xp[q * TOK : (q + 1) * TOK, 256 + h * 128 : 256 + (h + 1) * 128] = moved[:, 128:256]
 
-    hear(0)
-    tell(1)
-
     scaled = (sel[...] * gate).astype(BF)
 
     @pl.loop(0, NC)
@@ -214,8 +214,14 @@
         put(gs, c, dot(scaled, ogv[c]))
         own_block(gs, gr, c)
 
-    hear(1)
-    tell(2)
+    def rows_out(first, last):
+        @pl.loop(first, last)
+        def _(c):
+            send(gs, gr, osend, orecv, c)
+
+    rows_out(0, EARLY)
+    hear(2)
+    tell(3)
 
     gsum[...] = jnp.zeros_like(gsum)
 
@@ -251,9 +257,7 @@
 
     around(term_both)
     term_to(me, 1 - core)
-
-    hear(2)
-    tell(3)
+    rows_out(EARLY, NC)
 
     part = p1r.at[pl.ds(0, 2 * E - 1)]
     pltpu.make_async_copy(part, part, r1).wait()
@@ -267,17 +271,13 @@
 
     @pl.loop(0, NZ - 1)
     def _(i):
-        k = (i + 1) // 2
-        dz = NZ // 2 + k * (1 - 2 * (i % 2))
-        to = (z + dz) % NZ
+        k = lax.div(i + 1, 2)
+        dz = NZ // 2 + k * (1 - 2 * lax.rem(i, 2))
+        to = lax.rem(z + dz, NZ)
         pltpu.make_async_remote_copy(
-            src_ref=zs.at[to // 2], dst_ref=zr.at[z], send_sem=s2, recv_sem=r2,
+            src_ref=zs.at[lax.div(to, 2)], dst_ref=zr.at[z], send_sem=s2, recv_sem=r2,
             device_id=(to * 2 + core, me), device_id_type=MESH,
         ).start()
-
-    @pl.loop(0, NC)
-    def _(c):
-        send(gs, gr, osend, orecv, c)
 
     acc[...] = jnp.zeros_like(acc)
 
@@ -290,6 +290,8 @@
     high = acc[...].astype(BF)
     low = (acc[...] - high.astype(F32)).astype(BF)
     gh_o[...] = (dot(back, high) + dot(back, low)).astype(BF)
+    sent(vs, vsend)
+    sent(gs, osend)
 
     part = zr.at[pl.ds(0, NZ - 1)]
     pltpu.make_async_copy(part, part, r2).wait()
@@ -298,8 +300,6 @@
         column = column + zr[i]
     gc_o[...] = jnp.where(z % 2 == 0, column[:, 0:OUT], column[:, HALF : HALF + OUT])
 
-    sent(vs, vsend)
-    sent(gs, osend)
     part = p1r.at[pl.ds(0, 2 * E - 1)]
     pltpu.make_async_copy(part, part, s1).wait()
     part = zr.at[pl.ds(0, NZ - 1)]
@@ -312,13 +312,14 @@
     hbm = pl.BlockSpec(memory_space=pl.ANY)
     here = pl.BlockSpec(memory_space=pltpu.VMEM)
     block = (NC, E, HEAD, BW)
-    grad_hidden, grad_logit, grad_centroid = pl.pallas_call(
+    shapes = (
+        jax.ShapeDtypeStruct((CAP * E, FF), BF),
+        jax.ShapeDtypeStruct((8, TOK), F32),
+        jax.ShapeDtypeStruct((1, OUT), F32),
+    )
+    results = pl.pallas_call(
         kernel,
-        out_shape=(
-            jax.ShapeDtypeStruct((CAP * E, FF), BF),
-            jax.ShapeDtypeStruct((8, TOK), F32),
-            jax.ShapeDtypeStruct((1, OUT), F32),
-        ),
+        out_shape=tuple(pltpu.VMEM(s.shape, s.dtype) for s in shapes),
         in_specs=[hbm] * 7,
         out_specs=(here, here, here),
         scratch_shapes=[
@@ -336,6 +337,7 @@
             collective_id=0, has_side_effects=True, vmem_limit_bytes=56 * 1024 * 1024
         ),
     )(out_grad, router_input, down_weight[0], hidden, expert_ids.T, affinity.T, other_dgate.T)
+    grad_hidden, grad_logit, grad_centroid = results
     grad_hidden = grad_hidden.reshape(CAP, E, FF).transpose(1, 0, 2)[None, None]
     return grad_hidden, grad_logit.T, grad_centroid
 

time: 65.9 us -> 60.4 us (0.917)
  Pallas kernels: 60.9 us -> 57.8 us
  local copies, waits for them, and re-layouts: 4.11 us -> 1.83 us
    pallas_call x1, Pallas kernels: 60.9 us -> 57.8 us  [body(): pl.pallas_call(kernel, out_shape=tuple((pltpu.VMEM(s.shape, s.dtype) for...]
    unnamed x3, local copies, waits for them, and re-layouts: 4.11 us -> 1.83 us
where the time goes in v2:
time: 60.4 us; the launch traced here: 60.3 us
  Pallas kernels  57.8 us (96%)
  local copies, waits for them, and re-layouts  1.83 us (3%)
  between operations  0.64 us (1%)
    pallas_call x1, Pallas kernels, body(): pl.pallas_call(kernel, out_shape=tuple((pltpu.VMEM(s.shape, s.dtype) for...  57.8 us
    unnamed x3, local copies, waits for them, and re-layouts  1.83 us

profile of v2, /device:TPU:1, one launch (start us, length us, event | category | flops | bytes accessed | tf_op | source)
XLA Modules:
  0.0 60.3 jit_solution(4635309445642465130)
XLA Ops:
  0.6 57.8 %shard_map.94 = (bf16[160,1024]{1,0:T(8,128)(2,1)S(1)}, f32[8,128]{1,0:T(8,128)S(1)}, f32[1,56]{1,0:T(1,128)S(1)}) custom-call(bf16[128,3584]{1,0:T(8,128)(2,1)} %og_h.1, bf16[128,3584]{1,0:T(8,128)(2,1)} %ri_h.1, bf16[1024,3584]{1,0:T(8,128)(2,1)} %bitcast.17, bf16[160,1024]{1,0:T(8,128)(2,1)} %bitcast.18, s32[1,128]{1,0:T(1,128)} %bitcast.21, ...), custom_call_target="tpu_custom_call" | custom-call | tf_op jit(solution)/shard_map/pallas_call | solution.py:320
  58.5 0.7 %copy.13 = bf16[1,1,16,10,1024]{4,2,3,1,0:T(8,128)(2,1)} copy(bf16[1,1,16,10,1024]{4,2,3,1,0:T(8,128)(2,1)S(1)} %bitcast.15) | data formatting | bytes 655360
  59.2 0.6 copy.14
  59.8 0.5 copy.15

commit v3 on v2

--- a/solution.py
+++ b/solution.py
@@ -26,6 +26,7 @@
 OUT = 56
 HALF = 64
 EARLY = 2
+MID = 4
 
 _HOP = (0, 1, 2, 1)
 _ORDER = sorted(
@@ -58,7 +59,7 @@
     gh_o, gl_o, gc_o,
     wv, ogv, riv, hidv, idv, affv, othv,
     hp, sel, gsum, acc, vs, vr, gs, gr, xp, p1s, p1r, zs, zr,
-    wsem, lsem, vsend, vrecv, osend, orecv, s1, r1, s2, r2, up, down,
+    wsem, lsem, vsend, vrecv, osend, orecv, s1, r1, s2, r2, up, down, pair,
 ):
     dp = lax.axis_index("dp")
     me = lax.axis_index("expert")
@@ -81,29 +82,31 @@
         pltpu.make_async_copy(s, d, lsem.at[i])
         for i, (s, d) in enumerate(((ids_h, idv), (aff_h, affv), (oth_h, othv), (hid_h, hidv), (ri_h, riv)))
     ]
-    for copy in small[:4]:
-        copy.start()
-
     def w_copy(c):
         return pltpu.make_async_copy(w_h.at[:, pl.ds(c * CW, CW)], wv.at[c], wsem.at[c])
 
     def og_copy(c):
         return pltpu.make_async_copy(og_h.at[:, pl.ds(c * CW, CW)], ogv.at[c], wsem.at[NC + c])
 
-    for c in range(NC):
+    small[3].start()
+    w_copy(0).start()
+
+    barrier = pltpu.get_barrier_semaphore()
+    sibling = z * 2 + 1 - core
+
+    def greet(dp, e):
+        pl.semaphore_signal(barrier, inc=1, device_id=(dp, e), device_id_type=MESH)
+
+    for e in others:
+        greet(dp, e)
+    greet(sibling, me)
+    greet(level(1), me)
+    greet(level(NZ - 1), me)
+
+    for c in range(1, NC):
         w_copy(c).start()
-
-    barrier = pltpu.get_barrier_semaphore()
-
-    def greet(e):
-        pl.semaphore_signal(barrier, inc=1, device_id=(dp, e), device_id_type=MESH)
-        pl.semaphore_signal(barrier, inc=1, device_id=(z * 2 + 1 - core, e), device_id_type=MESH)
-
-    around(greet)
-    pl.semaphore_signal(barrier, inc=1, device_id=(z * 2 + 1 - core, me), device_id_type=MESH)
-    for dz in (1, NZ - 1):
-        pl.semaphore_signal(barrier, inc=1, device_id=(level(dz), me), device_id_type=MESH)
-
+    for copy in small[:3]:
+        copy.start()
     for c in range(NC):
         og_copy(c).start()
     small[4].start()
@@ -162,8 +165,9 @@
         pl.semaphore_wait(down.at[i], 1)
 
     make_v(0)
-    pl.semaphore_wait(barrier, 2 * (E - 1) + 3)
+    pl.semaphore_wait(barrier, E + 2)
     send(vs, vr, vsend, vrecv, 0)
+    pl.semaphore_signal(pair, inc=1, device_id=(sibling, me), device_id_type=MESH)
 
     tell(0)
 
@@ -255,9 +259,10 @@
         term_to(e, core)
         term_to(e, 1 - core)
 
+    pl.semaphore_wait(pair, 1)
     around(term_both)
     term_to(me, 1 - core)
-    rows_out(EARLY, NC)
+    rows_out(EARLY, MID)
 
     part = p1r.at[pl.ds(0, 2 * E - 1)]
     pltpu.make_async_copy(part, part, r1).wait()
@@ -279,6 +284,8 @@
             device_id=(to * 2 + core, me), device_id_type=MESH,
         ).start()
 
+    rows_out(MID, NC)
+
     acc[...] = jnp.zeros_like(acc)
 
     @pl.loop(0, NC)
@@ -304,6 +311,14 @@
     pltpu.make_async_copy(part, part, s1).wait()
     part = zr.at[pl.ds(0, NZ - 1)]
     pltpu.make_async_copy(part, part, s2).wait()
+
+
+def hand_over(a, b, c, a_o, b_o, c_o, sem):
+    copies = [pltpu.make_async_copy(s, d, sem.at[i]) for i, (s, d) in enumerate(((a, a_o), (b, b_o), (c, c_o)))]
+    for copy in copies:
+        copy.start()
+    for copy in copies:
+        copy.wait()
 
 
 def body(out_grad, router_input, down_weight, saved_hidden, expert_ids, affinity, other_dgate):
@@ -331,13 +346,19 @@
             vmem((2, E, 8, 256), BF), vmem((2 * E, 8, 256), BF),
             vmem((NZ // 2, 1, 128), F32), vmem((NZ, 1, 128), F32),
             dma((2 * NC,)), dma((5,)), dma, dma((NC,)), dma, dma((NC,)), dma, dma, dma, dma,
-            pltpu.SemaphoreType.REGULAR((4,)), pltpu.SemaphoreType.REGULAR((4,)),
+            pltpu.SemaphoreType.REGULAR((4,)), pltpu.SemaphoreType.REGULAR((4,)), pltpu.SemaphoreType.REGULAR,
         ],
         compiler_params=pltpu.CompilerParams(
             collective_id=0, has_side_effects=True, vmem_limit_bytes=56 * 1024 * 1024
         ),
     )(out_grad, router_input, down_weight[0], hidden, expert_ids.T, affinity.T, other_dgate.T)
-    grad_hidden, grad_logit, grad_centroid = results
+    grad_hidden, grad_logit, grad_centroid = pl.pallas_call(
+        hand_over,
+        out_shape=shapes,
+        in_specs=[here] * 3,
+        out_specs=(hbm, hbm, hbm),
+        scratch_shapes=[dma((3,))],
+    )(*(pltpu.with_memory_space_constraint(a, pltpu.VMEM) for a in results))
     grad_hidden = grad_hidden.reshape(CAP, E, FF).transpose(1, 0, 2)[None, None]
     return grad_hidden, grad_logit.T, grad_centroid
 

time: 60.4 us -> 58.7 us (0.972)
  local copies, waits for them, and re-layouts: 1.83 us -> 0 us
    unnamed x3 -> x0, local copies, waits for them, and re-layouts: 1.83 us -> none
    pallas_call x0 -> x1, Pallas kernels: none -> 0.76 us  [body(): pl.pallas_call(hand_over, out_shape=shapes, in_specs=[here] * 3, out_spec...]
    pallas_call x1, Pallas kernels: 57.8 us -> 57.1 us  [body(): pl.pallas_call(kernel, out_shape=tuple((pltpu.VMEM(s.shape, s.dtype) for...]
where the time goes in v3:
time: 58.7 us; the launch traced here: 58.5 us
  Pallas kernels  57.9 us (99%)
  between operations  0.64 us (1%)
    pallas_call x1, Pallas kernels, body(): pl.pallas_call(kernel, out_shape=tuple((pltpu.VMEM(s.shape, s.dtype) for...  57.1 us

profile of v3, /device:TPU:1, one launch (start us, length us, event | category | flops | bytes accessed | tf_op | source)
XLA Modules:
  0.0 58.5 jit_solution(4400265214838504833)
XLA Ops:
  0.6 57.1 %shard_map.94 = (bf16[160,1024]{1,0:T(8,128)(2,1)S(1)}, f32[8,128]{1,0:T(8,128)S(1)}, f32[1,56]{1,0:T(1,128)S(1)}) custom-call(bf16[128,3584]{1,0:T(8,128)(2,1)} %og_h.1, bf16[128,3584]{1,0:T(8,128)(2,1)} %ri_h.1, bf16[1024,3584]{1,0:T(8,128)(2,1)} %bitcast.15, bf16[160,1024]{1,0:T(8,128)(2,1)} %bitcast.16, s32[1,128]{1,0:T(1,128)} %bitcast.19, ...), custom_call_target="tpu_custom_call" | custom-call | tf_op jit(solution)/shard_map/pallas_call | solution.py:335
  57.8 0.8 %shard_map.95 = (bf16[160,1024]{1,0:T(8,128)(2,1)}, f32[8,128]{1,0:T(8,128)}, f32[1,56]{1,0:T(1,128)}) custom-call(bf16[160,1024]{1,0:T(8,128)(2,1)S(1)} %get-tuple-element.9.a, f32[8,128]{1,0:T(8,128)S(1)} %get-tuple-element.10.b, f32[1,56]{1,0:T(1,128)S(1)} %get-tuple-element.11.c), custom_call_target="tpu_custom_call" | custom-call | tf_op jit(solution)/shard_map/pallas_call | solution.py:355

commit v4 on v3

--- a/solution.py
+++ b/solution.py
@@ -28,10 +28,9 @@
 EARLY = 2
 MID = 4
 
-_HOP = (0, 1, 2, 1)
-_ORDER = sorted(
-    [(dx, dy) for dy in range(SIDE) for dx in range(SIDE) if (dx, dy) != (0, 0)],
-    key=lambda o: -(_HOP[o[0]] + _HOP[o[1]]),
+_ORDER = (
+    (2, 2), (2, 1), (1, 2), (2, 3), (3, 2), (1, 1), (3, 3), (1, 3), (3, 1),
+    (2, 0), (0, 2), (1, 0), (0, 1), (3, 0), (0, 3),
 )
 
 
@@ -58,7 +57,7 @@
     og_h, ri_h, w_h, hid_h, ids_h, aff_h, oth_h,
     gh_o, gl_o, gc_o,
     wv, ogv, riv, hidv, idv, affv, othv,
-    hp, sel, gsum, acc, vs, vr, gs, gr, xp, p1s, p1r, zs, zr,
+    hp, sel, acc, vs, vr, gs, gr, xp, p1s, p1r, zs, zr,
     wsem, lsem, vsend, vrecv, osend, orecv, s1, r1, s2, r2, up, down, pair,
 ):
     dp = lax.axis_index("dp")
@@ -227,14 +226,12 @@
     hear(2)
     tell(3)
 
-    gsum[...] = jnp.zeros_like(gsum)
-
-    @pl.loop(0, NC)
-    def _(c):
+    def more_own(c, so_far):
         arrived(vr, vrecv, c)
-        gsum[...] += dot_t(get(vr, c), ogv[c])
-
-    own = jnp.sum(gsum[...] * sel[...], axis=0, keepdims=True)
+        found = dot_t(get(vr, c), ogv[c]) * sel[...]
+        return so_far + jnp.sum(found.reshape(ROWS // 8, 8, TOK), axis=0)
+
+    own = jnp.sum(lax.fori_loop(0, NC, more_own, jnp.zeros((8, TOK), F32)), axis=0, keepdims=True)
     dgate = jnp.concatenate([own, othv[...]], axis=0)
     weighted = jnp.sum(dgate * aff, axis=0, keepdims=True) / total
     grad_logit = ROUTE_SCALE / total * (dgate - weighted) * aff * (1.0 - aff)
@@ -340,7 +337,7 @@
         scratch_shapes=[
             vmem((NC, FF, CW), BF), vmem((NC, TOK, CW), BF), vmem((TOK, D), BF), vmem((CAP * E, FF), BF),
             vmem((1, TOK), I32), vmem((8, TOK), F32), vmem((7, TOK), F32),
-            vmem((ROWS, FF), BF), vmem((ROWS, TOK), F32), vmem((ROWS, TOK), F32), vmem((ROWS, FF), F32),
+            vmem((ROWS, FF), BF), vmem((ROWS, TOK), F32), vmem((ROWS, FF), F32),
             vmem(block, BF), vmem(block, BF), vmem(block, BF), vmem(block, BF),
             vmem((8 * TOK, 512), BF),
             vmem((2, E, 8, 256), BF), vmem((2 * E, 8, 256), BF),

time: 58.7 us -> 58.3 us (level)
  no operation moved by 1% of the time
where the time goes in v4:
time: 58.3 us; the launch traced here: 58.1 us
  Pallas kernels  57.5 us (99%)
  between operations  0.64 us (1%)
    pallas_call x1, Pallas kernels, body(): pl.pallas_call(kernel, out_shape=tuple((pltpu.VMEM(s.shape, s.dtype) for...  56.7 us

profile of v4, /device:TPU:1, one launch (start us, length us, event | category | flops | bytes accessed | tf_op | source)
XLA Modules:
  0.0 58.1 jit_solution(8506779116409134591)
XLA Ops:
  0.6 56.7 %shard_map.94 = (bf16[160,1024]{1,0:T(8,128)(2,1)S(1)}, f32[8,128]{1,0:T(8,128)S(1)}, f32[1,56]{1,0:T(1,128)S(1)}) custom-call(bf16[128,3584]{1,0:T(8,128)(2,1)} %og_h.1, bf16[128,3584]{1,0:T(8,128)(2,1)} %ri_h.1, bf16[1024,3584]{1,0:T(8,128)(2,1)} %bitcast.15, bf16[160,1024]{1,0:T(8,128)(2,1)} %bitcast.16, s32[1,128]{1,0:T(1,128)} %bitcast.19, ...), custom_call_target="tpu_custom_call" | custom-call | tf_op jit(solution)/shard_map/pallas_call | solution.py:332
  57.4 0.8 %shard_map.95 = (bf16[160,1024]{1,0:T(8,128)(2,1)}, f32[8,128]{1,0:T(8,128)}, f32[1,56]{1,0:T(1,128)}) custom-call(bf16[160,1024]{1,0:T(8,128)(2,1)S(1)} %get-tuple-element.9.a, f32[8,128]{1,0:T(8,128)S(1)} %get-tuple-element.10.b, f32[1,56]{1,0:T(1,128)S(1)} %get-tuple-element.11.c), custom_call_target="tpu_custom_call" | custom-call | tf_op jit(solution)/shard_map/pallas_call | solution.py:352
